TPU v7x, 1024 devices: a whole 4x8x16 slice. The times are simulated.
1024 devices in a mesh: node: 64 (over x, y, core), local: 16 (over z).
Axes of the slice: x: 4, y: 8, z: 16, core: 2. Of those that a mesh axis runs over, the one named last changes fastest.
Arguments:
- grad_out: bfloat16 [8192, 3584], P('node', 'local'), may hold values from -6 to 6
- expert_ids: int32 [8192, 8], P('node'), may hold values from 0 to 255, as said below
- gate_scores: float32 [8192, 8], P('node'), may hold values from 0.05 to 0.95
- saved_hidden: bfloat16 [64, 512, 4096], P('node', None, 'local'), may hold values from -0.625 to 0.625
- down_weight: bfloat16 [262144, 3584], P(('node', 'local')), may hold values from -0.1875 to 0.1875
- shared_weight: bfloat16 [2048, 3584], P(None, 'local'), may hold values from -0.125 to 0.125
Outputs:
- expert_grad: bfloat16 [64, 512, 4096], P('node', None, 'local')
- router_grad: float32 [8192, 8], P('node')
- shared_grad: bfloat16 [2048, 8192], P('local', 'node')
Inputs may be any that keep to these rules, and one draw needn't show every extreme that they name: `expert_ids`: each token names 8 different experts lying in exactly 4 different groups, at least one pick in each of them. Of the 128 tokens of one index of node, exactly 8 name each group.
All inputs are finite; a program needn't handle non-finite values.
Results may differ from a plain program's by a relative error of at most 0.0049.
Values may be sent and summed in bfloat16 or wider, within the bound.
No kernel may reach another device: no remote copies, remote signals or barrier semaphores. Data moves between devices by JAX's collectives and lax.ppermute only.
A program may use at most 32 MiB of HBM per device.

v0:
```python
import jax
import jax.numpy as jnp
from jax import lax
from jax.experimental import pallas as pl
from jax.experimental.pallas import tpu as pltpu
from jax.sharding import PartitionSpec as P

EXP_NODE = 4
LANES = 128
CLASSES = 4
KERNEL_VMEM = 8 << 20

route_scale = 2.5


def iota(shape, dim):
    return lax.broadcasted_iota(jnp.int32, shape, dim)


def as_bf16(mask):
    return mask.astype(jnp.float32).astype(jnp.bfloat16)


def across(left, right):
    return lax.dot_general(left, right, (((1,), (1,)), ((), ())), preferred_element_type=jnp.float32)


def pieces(value):
    high = value.astype(jnp.bfloat16)
    rest = value - high.astype(jnp.float32)
    middle = rest.astype(jnp.bfloat16)
    low = (rest - middle.astype(jnp.float32)).astype(jnp.bfloat16)
    return high, middle, low


def exact_dot(left, right):
    high, middle, low = (jnp.dot(piece, right, preferred_element_type=jnp.float32) for piece in pieces(left))
    return high + middle + low


def route_kernel(capacity, grad_ref, ids_ref, scores_ref, payload_ref, select_ref):
    width, tokens = grad_ref.shape
    rows, padded = payload_ref.shape
    top = ids_ref.shape[0]
    experts = rows // capacity * EXP_NODE
    ids = ids_ref[...]
    scores = scores_ref[...]
    group = iota((rows, tokens), 0) // capacity
    picked = ids // EXP_NODE
    hits = group == picked[0:1, :]
    for k in range(1, top):
        hits = hits | (group == picked[k:k + 1, :])
    hot = hits.astype(jnp.float32)
    before = as_bf16(iota((tokens, tokens), 0) < iota((tokens, tokens), 1))
    rank = jnp.dot(hot.astype(jnp.bfloat16), before, preferred_element_type=jnp.float32)
    slot = (iota((rows, tokens), 0) % capacity).astype(jnp.float32)
    select = jnp.where(rank == slot, hot, 0.0).astype(jnp.bfloat16)
    select_ref[...] = select
    totals = jnp.sum(scores, axis=0, keepdims=True)
    weights = (route_scale * scores / totals).astype(jnp.bfloat16).astype(jnp.float32)
    expert = iota((experts, tokens), 0)
    spread = jnp.zeros((experts, tokens), jnp.float32)
    for k in range(top):
        spread = spread + jnp.where(expert == ids[k:k + 1, :], weights[k:k + 1, :], 0.0)
    payload_ref[:, :width] = across(select, grad_ref[...]).astype(payload_ref.dtype)
    gates = across(select, spread.astype(jnp.bfloat16))
    own = iota((rows, experts), 0) // capacity == iota((rows, experts), 1) // EXP_NODE
    place = iota((experts, padded - width), 0) % EXP_NODE == iota((experts, padded - width), 1)
    gates = jnp.dot(
        jnp.where(own, gates, 0.0).astype(jnp.bfloat16), as_bf16(place), preferred_element_type=jnp.float32
    )
    payload_ref[:, width:] = gates.astype(payload_ref.dtype)


def spread_kernel(capacity, score_ref, shared_ref, out_ref):
    groups = score_ref.shape[0]
    copies, height, lanes = shared_ref.shape
    score = score_ref[...].reshape(groups, score_ref.shape[2])
    held = lanes // capacity
    repeat = as_bf16(iota((capacity, lanes), 0) == iota((capacity, lanes), 1) % capacity)
    own = iota((groups, lanes), 0) % held == iota((groups, lanes), 1) // capacity
    lines = []
    for piece in pieces(score):
        tiled = jnp.where(own, jnp.dot(piece, repeat, preferred_element_type=jnp.float32), 0.0)
        for j in range(groups // held):
            lines.append(jnp.sum(tiled[j * held:(j + 1) * held, :], axis=0, keepdims=True))
    filler = out_ref.shape[1] - height - len(lines)
    lines.append(jnp.zeros((filler, lanes), jnp.float32))
    flat = jnp.concatenate(lines, axis=0).astype(jnp.bfloat16)
    for z in range(copies):
        out_ref[z, :height, :] = shared_ref[z]
        out_ref[z, height:, :] = flat


def router_kernel(capacity, parts_ref, select_ref, ids_ref, scores_ref, out_ref, shared_ref):
    copies, _, lanes = parts_ref.shape
    height = shared_ref.shape[0] // 4
    rows, tokens = select_ref.shape
    lines = rows // lanes
    top = ids_ref.shape[0]
    shares = copies // EXP_NODE
    held = lanes // capacity
    for first in range(4):
        shared = parts_ref[first, :height, :].astype(jnp.float32)
        for z in range(first + 4, copies, 4):
            shared = shared + parts_ref[z, :height, :].astype(jnp.float32)
        start = (first % 2 * 2 + first // 2) * height
        shared_ref[start:start + height, :] = shared.astype(shared_ref.dtype)
    ids = ids_ref[...]
    scores = scores_ref[...]
    fold = iota((held, lanes), 0) == iota((held, lanes), 1) // capacity
    score = []
    for c in range(EXP_NODE):
        total = jnp.zeros((lines, lanes), jnp.float32)
        for q in range(shares):
            sent = parts_ref[c * shares + q, height:, :].astype(jnp.float32)
            total = total + (sent[:lines] + sent[lines:2 * lines] + sent[2 * lines:3 * lines])
        score.append(total)
    pick = iota((top, tokens), 0)
    line = iota((EXP_NODE * held, tokens), 0)
    expert = line % held * EXP_NODE + line // held
    contrib = jnp.zeros((top, tokens), jnp.float32)
    for j in range(lines):
        left = jnp.concatenate([jnp.where(fold, score[c][j:j + 1, :], 0.0) for c in range(EXP_NODE)], axis=0)
        found = exact_dot(left, select_ref[j * lanes:(j + 1) * lanes, :])
        for k in range(top):
            mine = jnp.where(expert + j * held * EXP_NODE == ids[k:k + 1, :], found, 0.0)
            contrib = contrib + jnp.where(pick == k, jnp.sum(mine, axis=0, keepdims=True), 0.0)
    totals = jnp.sum(scores, axis=0, keepdims=True)
    mean_term = jnp.sum(scores * contrib, axis=0, keepdims=True) / totals
    out_ref[...] = route_scale / totals * (contrib - mean_term) * scores * (1.0 - scores)


def swap_halves(part, count, bit):
    kept = lax.axis_index("local") // bit % 2
    halves = part.reshape(count, 2, -1, part.shape[2])
    given = lax.dynamic_index_in_dim(halves, 1 - kept, 1, keepdims=False).astype(jnp.bfloat16)
    swapped = lax.ppermute(given, "local", [(z, z ^ bit) for z in range(count)])
    return lax.dynamic_index_in_dim(halves, kept, 1, keepdims=False) + swapped.astype(jnp.float32)


def body(grad_out, expert_ids, gate_scores, saved_hidden, down_weight, shared_weight):
    node_count = lax.axis_size("node")
    local_count = lax.axis_size("local")
    rows_total = saved_hidden.shape[1]
    capacity = rows_total // node_count
    tokens, slice_width = grad_out.shape
    quarter_width = down_weight.shape[0]
    share_count = local_count // EXP_NODE
    class_width = slice_width * local_count // CLASSES
    padded = class_width + LANES
    own_expert = lax.axis_index("local") // share_count
    ids = expert_ids.T
    scores = gate_scores.T
    vmem = pl.BlockSpec(memory_space=pltpu.VMEM)
    small = pltpu.CompilerParams(vmem_limit_bytes=KERNEL_VMEM)

    groups = [list(range(j, local_count, CLASSES)) for j in range(CLASSES)]
    class_grad = lax.all_gather(grad_out.T, "local", axis=0, tiled=True, axis_index_groups=groups)
    payload, select = pl.pallas_call(
        lambda *refs: route_kernel(capacity, *refs),
        out_shape=(
            jax.ShapeDtypeStruct((rows_total, padded), jnp.bfloat16),
            jax.ShapeDtypeStruct((rows_total, tokens), jnp.bfloat16),
        ),
        compiler_params=pltpu.CompilerParams(vmem_limit_bytes=2 * KERNEL_VMEM),
    )(class_grad, ids, scores)
    payload, grad_late = lax.optimization_barrier((payload, grad_out))
    shared_part = lax.dot_general(
        shared_weight, grad_late, (((1,), (1,)), ((), ())), preferred_element_type=jnp.float32
    )
    shared_part = swap_halves(shared_part.reshape(local_count, -1, tokens), local_count, 1)
    shared_part = swap_halves(shared_part, local_count, 2).astype(jnp.bfloat16)
    received = lax.all_to_all(
        payload.reshape(node_count, capacity, padded), "node", split_axis=0, concat_axis=0, tiled=True
    ).reshape(rows_total, padded)
    received, shared_part = lax.optimization_barrier((received, shared_part))

    half = 4 * LANES
    lower, upper = received[:, :half], received[:, half:class_width]
    right = [(z, (z + 1) % local_count) for z in range(local_count)]
    left = [(z, (z - 1) % local_count) for z in range(local_count)]
    by_class = down_weight.reshape(quarter_width, -1, CLASSES, slice_width)
    by_class = by_class.transpose(2, 0, 1, 3).reshape(CLASSES, quarter_width, class_width)

    def partial(rows, shift, part):
        own_class = (lax.axis_index("local") + shift) % CLASSES
        weight = lax.dynamic_index_in_dim(by_class, own_class, 0, keepdims=False)
        weight = weight[:, half:] if part else weight[:, :half]
        return lax.dot_general(rows, weight, (((1,), (1,)), ((), ())), preferred_element_type=jnp.float32)

    lower_left = lax.ppermute(lower, "local", right)
    upper_right = lax.ppermute(upper, "local", left)
    hidden_grad = partial(lower, 0, 0) + partial(upper, 0, 1)
    lower, upper, hidden_grad = lax.optimization_barrier((lower, upper, hidden_grad))
    upper_left = lax.ppermute(upper, "local", right)
    lower_right = lax.ppermute(lower, "local", left)
    lower_far = lax.ppermute(lower_left, "local", right)
    upper_far = lax.ppermute(upper_right, "local", left)
    hidden_grad = hidden_grad + partial(lower_left, CLASSES - 1, 0)
    hidden_grad = hidden_grad + partial(upper_right, 1, 1)
    hidden_grad = hidden_grad + partial(upper_left, CLASSES - 1, 1)
    hidden_grad = hidden_grad + partial(lower_right, 1, 0)
    hidden_grad = hidden_grad + partial(lower_far, 2, 0)
    hidden_grad = hidden_grad + partial(upper_far, 2, 1)
    gate_column = lax.dynamic_slice_in_dim(received, class_width + own_expert, 1, 1).astype(jnp.float32)
    expert_grad = (
        (gate_column * hidden_grad).astype(jnp.bfloat16).reshape(1, rows_total, quarter_width)
    )
    slot_dots = jnp.sum(hidden_grad * saved_hidden[0].astype(jnp.float32), axis=1)

    returned = lax.all_to_all(
        slot_dots.reshape(node_count, 1, capacity), "node", split_axis=0, concat_axis=0, tiled=True
    )
    height = shared_part.shape[1]
    extra = (3 * rows_total // LANES + 15) // 16 * 16
    spread = pl.pallas_call(
        lambda *refs: spread_kernel(capacity, *refs),
        out_shape=jax.ShapeDtypeStruct((local_count, height + extra, tokens), jnp.bfloat16),
        in_specs=[vmem] * 2,
        out_specs=vmem,
        compiler_params=small,
    )(returned, shared_part)
    parts = lax.all_to_all(spread, "local", split_axis=0, concat_axis=0, tiled=True)
    router_grad, shared_grad = pl.pallas_call(
        lambda *refs: router_kernel(capacity, *refs),
        out_shape=(
            jax.ShapeDtypeStruct(scores.shape, jnp.float32),
            jax.ShapeDtypeStruct((4 * height, tokens), jnp.bfloat16),
        ),
        in_specs=[vmem] * 4,
        out_specs=(vmem, vmem),
        compiler_params=small,
    )(parts, select, ids, scores)
    return (expert_grad, router_grad.T, shared_grad)


def solution(mesh):
    return jax.shard_map(
        body,
        mesh=mesh,
        in_specs=(
            P("node", "local"),
            P("node", None),
            P("node", None),
            P("node", None, "local"),
            P(("node", "local"), None),
            P(None, "local"),
        ),
        out_specs=(P("node", None, "local"), P("node", None), P("local", "node")),
        check_vma=False,
    )
```

profile of v0, /device:TPU:2, one launch (start us, length us, event | category | flops | bytes accessed | tf_op | source)
XLA Modules:
  0.0 165.6 jit_solution(16178588122701032388)
XLA Ops:
  0.7 30.8 %all_gather.3.refs_0_ = bf16[896,128]{1,0:T(8,128)(2,1)S(1)} all-gather(bf16[224,128]{1,0:T(8,128)(2,1)} %bitcast.65), channel_id=1, replica_groups={{0,4,8,12},{1,5,9,13},{2,6,10,14},{3,7,11,15},{16,20,24,28},{17,21,25,2..., dimensions={0}, use_global_device_ids=true | all-gather | bytes 286720 | tf_op jit(solution)/shard_map/all_gather | solution.py:159
  32.8 1.9 %shard_map.85 = (bf16[512,1024]{1,0:T(8,128)(2,1)}, bf16[512,128]{1,0:T(8,128)(2,1)S(1)}) custom-call(bf16[896,128]{1,0:T(8,128)(2,1)S(1)} %all_gather.3.refs_0_, s32[8,128]{1,0:T(8,128)S(1)} %bitcast.50, f32[8,128]{1,0:T(8,128)S(1)} %bitcast.52), custom_call_target="tpu_custom_call" | custom-call | tf_op jit(solution)/shard_map/pallas_call | solution.py:160
  34.7 10.7 %all-to-all-start = ((bf16[64,8,1024]{2,1,0:T(8,128)(2,1)}), bf16[64,8,1024]{2,1,0:T(8,128)(2,1)S(1)}, u32[]{:S(2)}, u32[]{:S(2)}) async-start(bf16[64,8,1024]{2,1,0:T(8,128)(2,1)} %bitcast.3), calls=%async_computation | async-start | bytes 2097152 | tf_op jit(solution)/shard_map/all_to_all | solution.py:174
  45.8 1.3 copy.27
  47.1 1.8 %fusion.5 = bf16[16,64,128]{2,1,0:T(8,128)(2,1)} fusion(f32[16,2,64,128]{3,2,1,0:T(8,128)} %bitcast.61, s32[]{:T(128)S(6)} %select_n.79), kind=kLoop, calls=%fused_computation.17 | loop fusion | bytes 524292 | tf_op jit(solution)/shard_map/convert_element_type | solution.py:137
  48.9 3.1 %collective-permute-start = (bf16[16,64,128]{2,1,0:T(8,128)(2,1)}, bf16[16,64,128]{2,1,0:T(8,128)(2,1)S(1)}, u32[]{:S(2)}, u32[]{:S(2)}) collective-permute-start(bf16[16,64,128]{2,1,0:T(8,128)(2,1)} %fusion.5), channel_id=1, source_target_pairs={{0,1},{1,0},{2,3},{3,2},{4,5},{5,4},{6,7},{7,6},{8,9},{9,8},{10,11... | collective-permute-start | bytes 786440 | tf_op jit(solution)/shard_map/ppermute | solution.py:138
  52.1 3.8 %copy.29 = bf16[256,3584]{0,1:T(8,128)(2,1)} copy(bf16[256,3584]{1,0:T(8,128)(2,1)} %param.10) | data formatting | bytes 3670016 | tf_op args[4]
  55.9 3.0 %copy.30 = bf16[4,256,4,224]{1,3,2,0:T(8,128)(2,1)} copy(bf16[4,256,4,224]{1,3,0,2:T(8,128)(2,1)} %bitcast.60) | data formatting | bytes 3670016 | tf_op jit(solution)/shard_map/transpose | solution.py:184
  59.4 4.9 %collective-permute-start.1 = (bf16[16,32,128]{2,1,0:T(8,128)(2,1)S(1)}, bf16[16,32,128]{2,1,0:T(8,128)(2,1)S(1)}, u32[]{:S(2)}, u32[]{:S(2)}) collective-permute-start(bf16[16,32,128]{2,1,0:T(8,128)(2,1)S(1)} %fusion.21), channel_id=1, source_target_pairs={{0,2},{1,3},{2,0},{3,1},{4,6},{5,7},{6,4},{7,5},{8,10},{9,11},{10,... | collective-permute-start | bytes 393224 | tf_op jit(solution)/shard_map/ppermute | solution.py:138
  64.4 2.6 %dynamic-slice_bitcast_fusion.2 = (bf16[256,896]{0,1:T(8,128)(2,1)}, bf16[256,896]{0,1:T(8,128)(2,1)}, bf16[256,896]{0,1:T(8,128)(2,1)}, bf16[256,896]{0,1:T(8,128)(2,1)S(1)}) fusion(bf16[4,256,896]{1,2,0:T(8,128)(2,1)} %bitcast.59, s32[]{:T(128)S(6)} %select_n.89, s32[]{:T(128)S(6)} %select_n.93, s32[]{:T(128)S(6)} %select_n.91, s32[]{:T(128)S(6)} %select_n.87), kind=kLoop, calls=%fused_computation.15 | loop fusion | bytes 3670032 | tf_op jit(solution)/shard_map/jit(dynamic_index_in_dim)/squeeze | solution.py:188
  66.9 3.8 %collective-permute-done.1 = bf16[16,32,128]{2,1,0:T(8,128)(2,1)S(1)} collective-permute-done((bf16[16,32,128]{2,1,0:T(8,128)(2,1)S(1)}, bf16[16,32,128]{2,1,0:T(8,128)(2,1)S(1)}, u32[]{:S(2)}, u32[]{:S(2)}) %collective-permute-start.1) | collective-permute-done | bytes 131104 | tf_op jit(solution)/shard_map/ppermute | solution.py:138
  70.7 1.8 %all-to-all-done = bf16[64,8,1024]{2,1,0:T(8,128)(2,1)S(1)} async-done(((bf16[64,8,1024]{2,1,0:T(8,128)(2,1)}), bf16[64,8,1024]{2,1,0:T(8,128)(2,1)S(1)}, u32[]{:S(2)}, u32[]{:S(2)}) %all-to-all-start) | async-done | bytes 1048608 | tf_op jit(solution)/shard_map/all_to_all | solution.py:174
  74.5 7.4 %collective-permute-start.3 = (bf16[512,384]{1,0:T(8,128)(2,1)}, bf16[512,384]{1,0:T(8,128)(2,1)}, u32[]{:S(2)}, u32[]{:S(2)}) collective-permute-start(bf16[512,384]{1,0:T(8,128)(2,1)} %slice.31), channel_id=1, source_target_pairs={{0,15},{1,0},{2,1},{3,2},{4,3},{5,4},{6,5},{7,6},{8,7},{9,8},{10,9... | collective-permute-start | bytes 1179656 | tf_op jit(solution)/shard_map/ppermute | solution.py:193
  82.2 1.9 %collective-permute-start.4 = (bf16[512,384]{1,0:T(8,128)(2,1)}, bf16[512,384]{1,0:T(8,128)(2,1)}, u32[]{:S(2)}, u32[]{:S(2)}) collective-permute-start(bf16[512,384]{1,0:T(8,128)(2,1)} %slice.31), channel_id=1, source_target_pairs={{0,1},{1,2},{2,3},{3,4},{4,5},{5,6},{6,7},{7,8},{8,9},{9,10},{10,1... | collective-permute-start | bytes 1179656 | tf_op jit(solution)/shard_map/ppermute | solution.py:196
  84.1 5.1 %collective-permute-start.5 = (bf16[512,512]{1,0:T(8,128)(2,1)}, bf16[512,512]{1,0:T(8,128)(2,1)S(1)}, u32[]{:S(2)}, u32[]{:S(2)}) collective-permute-start(bf16[512,512]{1,0:T(8,128)(2,1)} %slice.30), channel_id=1, source_target_pairs={{0,15},{1,0},{2,1},{3,2},{4,3},{5,4},{6,5},{7,6},{8,7},{9,8},{10,9... | collective-permute-start | bytes 1572872 | tf_op jit(solution)/shard_map/ppermute | solution.py:197
  89.3 2.1 %collective-permute-start.2 = (bf16[512,512]{1,0:T(8,128)(2,1)}, bf16[512,512]{1,0:T(8,128)(2,1)S(1)}, u32[]{:S(2)}, u32[]{:S(2)}) collective-permute-start(bf16[512,512]{1,0:T(8,128)(2,1)} %slice.30), channel_id=1, source_target_pairs={{0,1},{1,2},{2,3},{3,4},{4,5},{5,6},{6,7},{7,8},{8,9},{9,10},{10,1... | collective-permute-start | bytes 1572872 | tf_op jit(solution)/shard_map/ppermute | solution.py:192
  91.6 5.4 %collective-permute-start.7 = (bf16[512,384]{1,0:T(8,128)(2,1)}, bf16[512,384]{1,0:T(8,128)(2,1)S(1)}, u32[]{:S(2)}, u32[]{:S(2)}) collective-permute-start(bf16[512,384]{1,0:T(8,128)(2,1)} %collective-permute-done.3), channel_id=1, source_target_pairs={{0,15},{1,0},{2,1},{3,2},{4,3},{5,4},{6,5},{7,6},{8,7},{9,8},{10,9... | collective-permute-start | bytes 1179656 | tf_op jit(solution)/shard_map/ppermute | solution.py:199
  98.3 1.3 fusion.16
  99.6 3.0 %collective-permute-done.5 = bf16[512,512]{1,0:T(8,128)(2,1)S(1)} collective-permute-done((bf16[512,512]{1,0:T(8,128)(2,1)}, bf16[512,512]{1,0:T(8,128)(2,1)S(1)}, u32[]{:S(2)}, u32[]{:S(2)}) %collective-permute-start.5) | collective-permute-done | bytes 524320 | tf_op jit(solution)/shard_map/ppermute | solution.py:197
  103.9 4.7 %collective-permute-done.2 = bf16[512,512]{1,0:T(8,128)(2,1)S(1)} collective-permute-done((bf16[512,512]{1,0:T(8,128)(2,1)}, bf16[512,512]{1,0:T(8,128)(2,1)S(1)}, u32[]{:S(2)}, u32[]{:S(2)}) %collective-permute-start.2) | collective-permute-done | bytes 524320 | tf_op jit(solution)/shard_map/ppermute | solution.py:192
  108.6 1.9 %collective-permute-start.6 = (bf16[512,512]{1,0:T(8,128)(2,1)S(1)}, bf16[512,512]{1,0:T(8,128)(2,1)S(1)}, u32[]{:S(2)}, u32[]{:S(2)}) collective-permute-start(bf16[512,512]{1,0:T(8,128)(2,1)S(1)} %collective-permute-done.2), channel_id=1, source_target_pairs={{0,1},{1,2},{2,3},{3,4},{4,5},{5,6},{6,7},{7,8},{8,9},{9,10},{10,1... | collective-permute-start | bytes 1572872 | tf_op jit(solution)/shard_map/ppermute | solution.py:198
  111.3 14.3 %collective-permute-done.6 = bf16[512,512]{1,0:T(8,128)(2,1)S(1)} collective-permute-done((bf16[512,512]{1,0:T(8,128)(2,1)S(1)}, bf16[512,512]{1,0:T(8,128)(2,1)S(1)}, u32[]{:S(2)}, u32[]{:S(2)}) %collective-permute-start.6) | collective-permute-done | bytes 524320 | tf_op jit(solution)/shard_map/ppermute | solution.py:198
  126.7 14.6 %all_to_all.15.refs_0_ = f32[64,1,8]{2,1,0:T(1,128)S(1)} all-to-all(f32[64,1,8]{2,1,0:T(1,128)S(1)} %bitcast.66), channel_id=1, replica_groups=mesh['node'=64,'local'=16] {'node'}, dimensions={0} | all-to-all | bytes 4096 | tf_op jit(solution)/shard_map/all_to_all | solution.py:212
  141.6 23.0 %all_to_all.16.refs_0_ = bf16[16,48,128]{2,1,0:T(8,128)(2,1)S(1)} all-to-all(bf16[16,48,128]{2,1,0:T(8,128)(2,1)S(1)} %shard_map.86), channel_id=1, replica_groups=mesh['node'=64,'local'=16] {'local'}, dimensions={0} | all-to-all | bytes 393216 | tf_op jit(solution)/shard_map/all_to_all | solution.py:224
  (41 shorter events, 10.5 us)
Async XLA Ops:
  0.6 44.8 %copy-start = (bf16[2048,224]{0,1:T(8,128)(2,1)S(1)}, bf16[2048,224]{0,1:T(8,128)(2,1)}, u32[]{:S(2)}) copy-start(bf16[2048,224]{0,1:T(8,128)(2,1)} %param.11) | copy-start | bytes 2752516
  0.6 44.8 %copy-start.9 = (bf16[128,224]{0,1:T(8,128)(2,1)S(1)}, bf16[128,224]{0,1:T(8,128)(2,1)}, u32[]{:S(2)}) copy-start(bf16[128,224]{0,1:T(8,128)(2,1)} %param.6) | copy-start | bytes 172036
  31.5 0.7 copy-start.1
  32.2 0.7 copy-start.3
  34.7 37.8 %all-to-all-start = ((bf16[64,8,1024]{2,1,0:T(8,128)(2,1)}), bf16[64,8,1024]{2,1,0:T(8,128)(2,1)S(1)}, u32[]{:S(2)}, u32[]{:S(2)}) async-start(bf16[64,8,1024]{2,1,0:T(8,128)(2,1)} %bitcast.3), calls=%async_computation | async-start | bytes 2097152 | tf_op jit(solution)/shard_map/all_to_all | solution.py:174
  48.9 10.5 %collective-permute-start = (bf16[16,64,128]{2,1,0:T(8,128)(2,1)}, bf16[16,64,128]{2,1,0:T(8,128)(2,1)S(1)}, u32[]{:S(2)}, u32[]{:S(2)}) collective-permute-start(bf16[16,64,128]{2,1,0:T(8,128)(2,1)} %fusion.5), channel_id=1, source_target_pairs={{0,1},{1,0},{2,3},{3,2},{4,5},{5,4},{6,7},{7,6},{8,9},{9,8},{10,11... | collective-permute-start | bytes 786440 | tf_op jit(solution)/shard_map/ppermute | solution.py:138
  55.9 3.5 %copy-start.5 = (f32[2048,128]{1,0:T(8,128)S(1)}, f32[2048,128]{1,0:T(8,128)}, u32[]{:S(2)}) copy-start(f32[2048,128]{1,0:T(8,128)} %copy.27) | copy-start | bytes 3145732
  59.4 11.3 %collective-permute-start.1 = (bf16[16,32,128]{2,1,0:T(8,128)(2,1)S(1)}, bf16[16,32,128]{2,1,0:T(8,128)(2,1)S(1)}, u32[]{:S(2)}, u32[]{:S(2)}) collective-permute-start(bf16[16,32,128]{2,1,0:T(8,128)(2,1)S(1)} %fusion.21), channel_id=1, source_target_pairs={{0,2},{1,3},{2,0},{3,1},{4,6},{5,7},{6,4},{7,5},{8,10},{9,11},{10,... | collective-permute-start | bytes 393224 | tf_op jit(solution)/shard_map/ppermute | solution.py:138
  74.5 17.1 %collective-permute-start.3 = (bf16[512,384]{1,0:T(8,128)(2,1)}, bf16[512,384]{1,0:T(8,128)(2,1)}, u32[]{:S(2)}, u32[]{:S(2)}) collective-permute-start(bf16[512,384]{1,0:T(8,128)(2,1)} %slice.31), channel_id=1, source_target_pairs={{0,15},{1,0},{2,1},{3,2},{4,3},{5,4},{6,5},{7,6},{8,7},{9,8},{10,9... | collective-permute-start | bytes 1179656 | tf_op jit(solution)/shard_map/ppermute | solution.py:193
  82.2 16.1 %collective-permute-start.4 = (bf16[512,384]{1,0:T(8,128)(2,1)}, bf16[512,384]{1,0:T(8,128)(2,1)}, u32[]{:S(2)}, u32[]{:S(2)}) collective-permute-start(bf16[512,384]{1,0:T(8,128)(2,1)} %slice.31), channel_id=1, source_target_pairs={{0,1},{1,2},{2,3},{3,4},{4,5},{5,6},{6,7},{7,8},{8,9},{9,10},{10,1... | collective-permute-start | bytes 1179656 | tf_op jit(solution)/shard_map/ppermute | solution.py:196
  84.1 18.5 %collective-permute-start.5 = (bf16[512,512]{1,0:T(8,128)(2,1)}, bf16[512,512]{1,0:T(8,128)(2,1)S(1)}, u32[]{:S(2)}, u32[]{:S(2)}) collective-permute-start(bf16[512,512]{1,0:T(8,128)(2,1)} %slice.30), channel_id=1, source_target_pairs={{0,15},{1,0},{2,1},{3,2},{4,3},{5,4},{6,5},{7,6},{8,7},{9,8},{10,9... | collective-permute-start | bytes 1572872 | tf_op jit(solution)/shard_map/ppermute | solution.py:197
  89.3 21.2 %copy-start.7 = (bf16[256,896]{0,1:T(8,128)(2,1)S(1)}, bf16[256,896]{0,1:T(8,128)(2,1)}, u32[]{:S(2)}) copy-start(bf16[256,896]{0,1:T(8,128)(2,1)} %get-tuple-element.25) | copy-start | bytes 1376260
  89.3 19.3 %collective-permute-start.2 = (bf16[512,512]{1,0:T(8,128)(2,1)}, bf16[512,512]{1,0:T(8,128)(2,1)S(1)}, u32[]{:S(2)}, u32[]{:S(2)}) collective-permute-start(bf16[512,512]{1,0:T(8,128)(2,1)} %slice.30), channel_id=1, source_target_pairs={{0,1},{1,2},{2,3},{3,4},{4,5},{5,6},{6,7},{7,8},{8,9},{9,10},{10,1... | collective-permute-start | bytes 1572872 | tf_op jit(solution)/shard_map/ppermute | solution.py:192
  91.6 19.4 %collective-permute-start.7 = (bf16[512,384]{1,0:T(8,128)(2,1)}, bf16[512,384]{1,0:T(8,128)(2,1)S(1)}, u32[]{:S(2)}, u32[]{:S(2)}) collective-permute-start(bf16[512,384]{1,0:T(8,128)(2,1)} %collective-permute-done.3), channel_id=1, source_target_pairs={{0,15},{1,0},{2,1},{3,2},{4,3},{5,4},{6,5},{7,6},{8,7},{9,8},{10,9... | collective-permute-start | bytes 1179656 | tf_op jit(solution)/shard_map/ppermute | solution.py:199
  103.8 7.2 %copy-start.6 = (bf16[256,896]{0,1:T(8,128)(2,1)S(1)}, bf16[256,896]{0,1:T(8,128)(2,1)}, u32[]{:S(2)}) copy-start(bf16[256,896]{0,1:T(8,128)(2,1)} %get-tuple-element.26) | copy-start | bytes 1376260
  103.8 21.8 %copy-start.8 = (bf16[1,512,256]{2,1,0:T(8,128)(2,1)S(1)}, bf16[1,512,256]{2,1,0:T(8,128)(2,1)}, u32[]{:S(2)}) copy-start(bf16[1,512,256]{2,1,0:T(8,128)(2,1)} %param.9) | copy-start | bytes 786436
  108.6 17.0 %collective-permute-start.6 = (bf16[512,512]{1,0:T(8,128)(2,1)S(1)}, bf16[512,512]{1,0:T(8,128)(2,1)S(1)}, u32[]{:S(2)}, u32[]{:S(2)}) collective-permute-start(bf16[512,512]{1,0:T(8,128)(2,1)S(1)} %collective-permute-done.2), channel_id=1, source_target_pairs={{0,1},{1,2},{2,3},{3,4},{4,5},{5,6},{6,7},{7,8},{8,9},{9,10},{10,1... | collective-permute-start | bytes 1572872 | tf_op jit(solution)/shard_map/ppermute | solution.py:198
  111.3 53.3 %copy-start.2 = (s32[128,8]{0,1:T(8,128)S(1)}, s32[128,8]{0,1:T(8,128)}, u32[]{:S(2)}) copy-start(s32[128,8]{0,1:T(8,128)} %param.7) | copy-start | bytes 12292
  111.3 53.3 %copy-start.4 = (f32[128,8]{0,1:T(8,128)S(1)}, f32[128,8]{0,1:T(8,128)}, u32[]{:S(2)}) copy-start(f32[128,8]{0,1:T(8,128)} %param.8) | copy-start | bytes 12292
where the time goes:
time: 166 us
  blocking collectives  68.4 us (41%)
  starting transfers between devices  42.5 us (26%)
  waiting for transfers between devices  28.2 us (17%)
  local copies, waits for them, and re-layouts  15.6 us (9%)
  matrix products  6.44 us (4%)
  Pallas kernels  3.14 us (2%)
    all_gather x1, blocking collectives, body(): lax.all_gather(grad_out.T, 'local', axis=0, tiled=True, axis_index_groups...  30.8 us
    all_to_all x1, blocking collectives, body(): lax.all_to_all(spread, 'local', split_axis=0, concat_axis=0, tiled=True)  23 us
    all_to_all x1, blocking collectives, body(): lax.all_to_all(slot_dots.reshape(node_count, 1, capacity), 'node', split_...  14.6 us
    ppermute x1, waiting for transfers between devices, body(): lower_far = lax.ppermute(lower_left, 'local', right)  14.3 us
    all_to_all x1, starting transfers between devices, body(): lax.all_to_all(payload.reshape(node_count, capacity, padded), 'node', spl...  10.7 us
    ppermute x2, starting transfers between devices, swap_halves(): swapped = lax.ppermute(given, 'local', [(z, z ^ bit) for z in range(count)])  8.04 us
    ppermute x1, starting transfers between devices, body(): upper_right = lax.ppermute(upper, 'local', left)  7.44 us
    dot_general x8, matrix products, partial(): lax.dot_general(rows, weight, (((1,), (1,)), ((), ())), preferred_element...  6.1 us
  transfers between devices with their start and end apart: 9, of which 7 were waited for; matrix products, arithmetic and copies ran while one was open for 11% of the time, Pallas kernels for 0%

commit v1 on v0

--- a/solution.py
+++ b/solution.py
@@ -177,11 +177,12 @@
     received, shared_part = lax.optimization_barrier((received, shared_part))
 
     half = 4 * LANES
-    lower, upper = received[:, :half], received[:, half:class_width]
+    lower, upper = received[:, :half], received[:, half:]
     right = [(z, (z + 1) % local_count) for z in range(local_count)]
     left = [(z, (z - 1) % local_count) for z in range(local_count)]
     by_class = down_weight.reshape(quarter_width, -1, CLASSES, slice_width)
     by_class = by_class.transpose(2, 0, 1, 3).reshape(CLASSES, quarter_width, class_width)
+    by_class = jnp.pad(by_class, ((0, 0), (0, 0), (0, padded - class_width)))
 
     def partial(rows, shift, part):
         own_class = (lax.axis_index("local") + shift) % CLASSES

time: 166 us -> 163 us (0.982)
  waiting for transfers between devices: 28.2 us -> 22.8 us
  matrix products: 6.44 us -> 8.45 us
    ppermute x1, waiting for transfers between devices: 14.3 us -> 5.38 us  [body(): lower_far = lax.ppermute(lower_left, 'local', right)]
    ppermute x1, waiting for transfers between devices: 4.73 us -> 0.21 us  [body(): lower_left = lax.ppermute(lower, 'local', right)]
    ppermute x1, waiting for transfers between devices: 0.01 us -> 4.47 us  [body(): upper_left = lax.ppermute(upper, 'local', right)]
    ppermute x1, waiting for transfers between devices: 0.19 us -> 2.68 us  [body(): upper_far = lax.ppermute(upper_right, 'local', left)]
    dot_general x8, matrix products: 6.1 us -> 8.12 us  [partial(): lax.dot_general(rows, weight, (((1,), (1,)), ((), ())), preferred_element...]
    ppermute x1, waiting for transfers between devices: 0.01 us -> 1.95 us  [body(): upper_right = lax.ppermute(upper, 'local', left)]
    unnamed x21 -> x23, local copies, waits for them, and re-layouts: 5.22 us -> 5.32 us
  transfers between devices with their start and end apart: 9 -> 9, of which waited for: 7 -> 9; matrix products, arithmetic and copies ran while one was open for 11% -> 12% of each run, Pallas kernels for 0% -> 0%
where the time goes in v1:
time: 163 us; the launch traced here: 162 us
  blocking collectives  68.7 us (42%)
  starting transfers between devices  42.6 us (26%)
  waiting for transfers between devices  22.8 us (14%)
  local copies, waits for them, and re-layouts  15.1 us (9%)
  matrix products  8.45 us (5%)
  Pallas kernels  3.13 us (2%)
    all_gather x1, blocking collectives, body(): lax.all_gather(grad_out.T, 'local', axis=0, tiled=True, axis_index_groups...  30.8 us
    all_to_all x1, blocking collectives, body(): lax.all_to_all(spread, 'local', split_axis=0, concat_axis=0, tiled=True)  23 us
    all_to_all x1, blocking collectives, body(): lax.all_to_all(slot_dots.reshape(node_count, 1, capacity), 'node', split_...  14.9 us
    all_to_all x1, starting transfers between devices, body(): lax.all_to_all(payload.reshape(node_count, capacity, padded), 'node', spl...  10.7 us
    dot_general x8, matrix products, partial(): lax.dot_general(rows, weight, (((1,), (1,)), ((), ())), preferred_element...  8.12 us
    ppermute x2, starting transfers between devices, swap_halves(): swapped = lax.ppermute(given, 'local', [(z, z ^ bit) for z in range(count)])  8.03 us
    ppermute x1, starting transfers between devices, body(): upper_right = lax.ppermute(upper, 'local', left)  7.44 us
    ppermute x1, starting transfers between devices, body(): upper_far = lax.ppermute(upper_right, 'local', left)  5.59 us
  transfers between devices with their start and end apart: 9, of which 9 were waited for; matrix products, arithmetic and copies ran while one was open for 12% of the time, Pallas kernels for 0%

profile of v1, /device:TPU:2, one launch (start us, length us, event | category | flops | bytes accessed | tf_op | source)
XLA Modules:
  0.0 162.1 jit_solution(3711599203199314397)
XLA Ops:
  0.7 30.8 %all_gather.3.refs_0_ = bf16[896,128]{1,0:T(8,128)(2,1)S(1)} all-gather(bf16[224,128]{1,0:T(8,128)(2,1)} %bitcast.64), channel_id=1, replica_groups={{0,4,8,12},{1,5,9,13},{2,6,10,14},{3,7,11,15},{16,20,24,28},{17,21,25,2..., dimensions={0}, use_global_device_ids=true | all-gather | bytes 286720 | tf_op jit(solution)/shard_map/all_gather | solution.py:159
  32.8 1.9 %shard_map.85 = (bf16[512,1024]{1,0:T(8,128)(2,1)}, bf16[512,128]{1,0:T(8,128)(2,1)S(1)}) custom-call(bf16[896,128]{1,0:T(8,128)(2,1)S(1)} %all_gather.3.refs_0_, s32[8,128]{1,0:T(8,128)S(1)} %bitcast.50, f32[8,128]{1,0:T(8,128)S(1)} %bitcast.52), custom_call_target="tpu_custom_call" | custom-call | tf_op jit(solution)/shard_map/pallas_call | solution.py:160
  34.7 10.7 %all-to-all-start = ((bf16[64,8,1024]{2,1,0:T(8,128)(2,1)}), bf16[64,8,1024]{2,1,0:T(8,128)(2,1)S(1)}, u32[]{:S(2)}, u32[]{:S(2)}) async-start(bf16[64,8,1024]{2,1,0:T(8,128)(2,1)} %bitcast.3), calls=%async_computation | async-start | bytes 2097152 | tf_op jit(solution)/shard_map/all_to_all | solution.py:174
  47.1 1.8 %fusion.9 = bf16[16,64,128]{2,1,0:T(8,128)(2,1)} fusion(f32[16,2,64,128]{3,2,1,0:T(8,128)} %bitcast.60, s32[]{:T(128)S(6)} %select_n.79), kind=kLoop, calls=%fused_computation.21 | loop fusion | bytes 524292 | tf_op jit(solution)/shard_map/convert_element_type | solution.py:137
  48.9 3.1 %collective-permute-start = (bf16[16,64,128]{2,1,0:T(8,128)(2,1)}, bf16[16,64,128]{2,1,0:T(8,128)(2,1)S(1)}, u32[]{:S(2)}, u32[]{:S(2)}) collective-permute-start(bf16[16,64,128]{2,1,0:T(8,128)(2,1)} %fusion.9), channel_id=1, source_target_pairs={{0,1},{1,0},{2,3},{3,2},{4,5},{5,4},{6,7},{7,6},{8,9},{9,8},{10,11... | collective-permute-start | bytes 786440 | tf_op jit(solution)/shard_map/ppermute | solution.py:138
  52.1 3.8 %copy.29 = bf16[256,3584]{0,1:T(8,128)(2,1)} copy(bf16[256,3584]{1,0:T(8,128)(2,1)} %param.10) | data formatting | bytes 3670016 | tf_op args[4]
  55.9 3.0 %copy.30 = bf16[4,256,4,224]{1,3,2,0:T(8,128)(2,1)} copy(bf16[4,256,4,224]{1,3,0,2:T(8,128)(2,1)} %bitcast.59) | data formatting | bytes 3670016 | tf_op jit(solution)/shard_map/transpose | solution.py:184
  59.4 4.9 %collective-permute-start.1 = (bf16[16,32,128]{2,1,0:T(8,128)(2,1)S(1)}, bf16[16,32,128]{2,1,0:T(8,128)(2,1)S(1)}, u32[]{:S(2)}, u32[]{:S(2)}) collective-permute-start(bf16[16,32,128]{2,1,0:T(8,128)(2,1)S(1)} %fusion.25), channel_id=1, source_target_pairs={{0,2},{1,3},{2,0},{3,1},{4,6},{5,7},{6,4},{7,5},{8,10},{9,11},{10,... | collective-permute-start | bytes 393224 | tf_op jit(solution)/shard_map/ppermute | solution.py:138
  64.4 2.5 %fusion.5 = (bf16[256,1024]{0,1:T(8,128)(2,1)}, bf16[256,1024]{0,1:T(8,128)(2,1)S(1)}, bf16[256,1024]{0,1:T(8,128)(2,1)S(1)}, bf16[256,1024]{0,1:T(8,128)(2,1)}) fusion(s32[]{:T(128)S(6)} %select_n.89, bf16[4,256,896]{1,2,0:T(8,128)(2,1)} %bitcast.58, s32[]{:T(128)S(6)} %select_n.91, s32[]{:T(128)S(6)} %select_n.93, s32[]{:T(128)S(6)} %select_n.87), kind=kLoop, calls=%fused_computation.13 | loop fusion | bytes 3932176 | tf_op jit(solution)/shard_map/jit(dynamic_index_in_dim)/squeeze | solution.py:189
  66.9 3.8 %collective-permute-done.1 = bf16[16,32,128]{2,1,0:T(8,128)(2,1)S(1)} collective-permute-done((bf16[16,32,128]{2,1,0:T(8,128)(2,1)S(1)}, bf16[16,32,128]{2,1,0:T(8,128)(2,1)S(1)}, u32[]{:S(2)}, u32[]{:S(2)}) %collective-permute-start.1) | collective-permute-done | bytes 131104 | tf_op jit(solution)/shard_map/ppermute | solution.py:138
  70.7 1.8 %all-to-all-done = bf16[64,8,1024]{2,1,0:T(8,128)(2,1)S(1)} async-done(((bf16[64,8,1024]{2,1,0:T(8,128)(2,1)}), bf16[64,8,1024]{2,1,0:T(8,128)(2,1)S(1)}, u32[]{:S(2)}, u32[]{:S(2)}) %all-to-all-start) | async-done | bytes 1048608 | tf_op jit(solution)/shard_map/all_to_all | solution.py:174
  74.0 7.4 %collective-permute-start.3 = (bf16[512,512]{1,0:T(8,128)(2,1)}, bf16[512,512]{1,0:T(8,128)(2,1)}, u32[]{:S(2)}, u32[]{:S(2)}) collective-permute-start(bf16[512,512]{1,0:T(8,128)(2,1)} %get-tuple-element.19), channel_id=1, source_target_pairs={{0,15},{1,0},{2,1},{3,2},{4,3},{5,4},{6,5},{7,6},{8,7},{9,8},{10,9... | collective-permute-start | bytes 1572872 | tf_op jit(solution)/shard_map/ppermute | solution.py:194
  81.4 1.9 %collective-permute-start.2 = (bf16[512,512]{1,0:T(8,128)(2,1)}, bf16[512,512]{1,0:T(8,128)(2,1)}, u32[]{:S(2)}, u32[]{:S(2)}) collective-permute-start(bf16[512,512]{1,0:T(8,128)(2,1)} %get-tuple-element.20), channel_id=1, source_target_pairs={{0,1},{1,2},{2,3},{3,4},{4,5},{5,6},{6,7},{7,8},{8,9},{9,10},{10,1... | collective-permute-start | bytes 1572872 | tf_op jit(solution)/shard_map/ppermute | solution.py:193
  84.5 5.1 %collective-permute-start.5 = (bf16[512,512]{1,0:T(8,128)(2,1)}, bf16[512,512]{1,0:T(8,128)(2,1)}, u32[]{:S(2)}, u32[]{:S(2)}) collective-permute-start(bf16[512,512]{1,0:T(8,128)(2,1)} %get-tuple-element.20), channel_id=1, source_target_pairs={{0,15},{1,0},{2,1},{3,2},{4,3},{5,4},{6,5},{7,6},{8,7},{9,8},{10,9... | collective-permute-start | bytes 1572872 | tf_op jit(solution)/shard_map/ppermute | solution.py:198
  89.6 1.9 %collective-permute-start.4 = (bf16[512,512]{1,0:T(8,128)(2,1)}, bf16[512,512]{1,0:T(8,128)(2,1)}, u32[]{:S(2)}, u32[]{:S(2)}) collective-permute-start(bf16[512,512]{1,0:T(8,128)(2,1)} %get-tuple-element.19), channel_id=1, source_target_pairs={{0,1},{1,2},{2,3},{3,4},{4,5},{5,6},{6,7},{7,8},{8,9},{9,10},{10,1... | collective-permute-start | bytes 1572872 | tf_op jit(solution)/shard_map/ppermute | solution.py:197
  91.7 1.9 %collective-permute-done.3 = bf16[512,512]{1,0:T(8,128)(2,1)} collective-permute-done((bf16[512,512]{1,0:T(8,128)(2,1)}, bf16[512,512]{1,0:T(8,128)(2,1)}, u32[]{:S(2)}, u32[]{:S(2)}) %collective-permute-start.3) | collective-permute-done | bytes 524320 | tf_op jit(solution)/shard_map/ppermute | solution.py:194
  93.7 5.6 %collective-permute-start.7 = (bf16[512,512]{1,0:T(8,128)(2,1)}, bf16[512,512]{1,0:T(8,128)(2,1)S(1)}, u32[]{:S(2)}, u32[]{:S(2)}) collective-permute-start(bf16[512,512]{1,0:T(8,128)(2,1)} %collective-permute-done.3), channel_id=1, source_target_pairs={{0,15},{1,0},{2,1},{3,2},{4,3},{5,4},{6,5},{7,6},{8,7},{9,8},{10,9... | collective-permute-start | bytes 1572872 | tf_op jit(solution)/shard_map/ppermute | solution.py:200
  99.5 1.9 %collective-permute-start.6 = (bf16[512,512]{1,0:T(8,128)(2,1)}, bf16[512,512]{1,0:T(8,128)(2,1)S(1)}, u32[]{:S(2)}, u32[]{:S(2)}) collective-permute-start(bf16[512,512]{1,0:T(8,128)(2,1)} %collective-permute-done.2), channel_id=1, source_target_pairs={{0,1},{1,2},{2,3},{3,4},{4,5},{5,6},{6,7},{7,8},{8,9},{9,10},{10,1... | collective-permute-start | bytes 1572872 | tf_op jit(solution)/shard_map/ppermute | solution.py:199
  102.8 2.1 %collective-permute-done.5 = bf16[512,512]{1,0:T(8,128)(2,1)} collective-permute-done((bf16[512,512]{1,0:T(8,128)(2,1)}, bf16[512,512]{1,0:T(8,128)(2,1)}, u32[]{:S(2)}, u32[]{:S(2)}) %collective-permute-start.5) | collective-permute-done | bytes 524320 | tf_op jit(solution)/shard_map/ppermute | solution.py:198
  106.3 4.5 %collective-permute-done.4 = bf16[512,512]{1,0:T(8,128)(2,1)} collective-permute-done((bf16[512,512]{1,0:T(8,128)(2,1)}, bf16[512,512]{1,0:T(8,128)(2,1)}, u32[]{:S(2)}, u32[]{:S(2)}) %collective-permute-start.4) | collective-permute-done | bytes 524320 | tf_op jit(solution)/shard_map/ppermute | solution.py:197
  113.5 2.7 %collective-permute-done.7 = bf16[512,512]{1,0:T(8,128)(2,1)S(1)} collective-permute-done((bf16[512,512]{1,0:T(8,128)(2,1)}, bf16[512,512]{1,0:T(8,128)(2,1)S(1)}, u32[]{:S(2)}, u32[]{:S(2)}) %collective-permute-start.7) | collective-permute-done | bytes 524320 | tf_op jit(solution)/shard_map/ppermute | solution.py:200
  116.5 5.4 %collective-permute-done.6 = bf16[512,512]{1,0:T(8,128)(2,1)S(1)} collective-permute-done((bf16[512,512]{1,0:T(8,128)(2,1)}, bf16[512,512]{1,0:T(8,128)(2,1)S(1)}, u32[]{:S(2)}, u32[]{:S(2)}) %collective-permute-start.6) | collective-permute-done | bytes 524320 | tf_op jit(solution)/shard_map/ppermute | solution.py:199
  123.0 14.9 %all_to_all.15.refs_0_ = f32[64,1,8]{2,1,0:T(1,128)S(1)} all-to-all(f32[64,1,8]{2,1,0:T(1,128)S(1)} %bitcast.65), channel_id=1, replica_groups=mesh['node'=64,'local'=16] {'node'}, dimensions={0} | all-to-all | bytes 4096 | tf_op jit(solution)/shard_map/all_to_all | solution.py:213
  138.1 23.0 %all_to_all.16.refs_0_ = bf16[16,48,128]{2,1,0:T(8,128)(2,1)S(1)} all-to-all(bf16[16,48,128]{2,1,0:T(8,128)(2,1)S(1)} %shard_map.86), channel_id=1, replica_groups=mesh['node'=64,'local'=16] {'local'}, dimensions={0} | all-to-all | bytes 393216 | tf_op jit(solution)/shard_map/all_to_all | solution.py:225
  (42 shorter events, 14.8 us)
Async XLA Ops:
  0.6 44.8 %copy-start = (bf16[2048,224]{0,1:T(8,128)(2,1)S(1)}, bf16[2048,224]{0,1:T(8,128)(2,1)}, u32[]{:S(2)}) copy-start(bf16[2048,224]{0,1:T(8,128)(2,1)} %param.11) | copy-start | bytes 2752516
  0.6 44.8 %copy-start.10 = (bf16[128,224]{0,1:T(8,128)(2,1)S(1)}, bf16[128,224]{0,1:T(8,128)(2,1)}, u32[]{:S(2)}) copy-start(bf16[128,224]{0,1:T(8,128)(2,1)} %param.6) | copy-start | bytes 172036
  31.5 0.7 copy-start.1
  32.2 0.7 copy-start.3
  34.7 37.8 %all-to-all-start = ((bf16[64,8,1024]{2,1,0:T(8,128)(2,1)}), bf16[64,8,1024]{2,1,0:T(8,128)(2,1)S(1)}, u32[]{:S(2)}, u32[]{:S(2)}) async-start(bf16[64,8,1024]{2,1,0:T(8,128)(2,1)} %bitcast.3), calls=%async_computation | async-start | bytes 2097152 | tf_op jit(solution)/shard_map/all_to_all | solution.py:174
  48.9 10.5 %collective-permute-start = (bf16[16,64,128]{2,1,0:T(8,128)(2,1)}, bf16[16,64,128]{2,1,0:T(8,128)(2,1)S(1)}, u32[]{:S(2)}, u32[]{:S(2)}) collective-permute-start(bf16[16,64,128]{2,1,0:T(8,128)(2,1)} %fusion.9), channel_id=1, source_target_pairs={{0,1},{1,0},{2,3},{3,2},{4,5},{5,4},{6,7},{7,6},{8,9},{9,8},{10,11... | collective-permute-start | bytes 786440 | tf_op jit(solution)/shard_map/ppermute | solution.py:138
  55.9 3.5 %copy-start.5 = (f32[2048,128]{1,0:T(8,128)S(1)}, f32[2048,128]{1,0:T(8,128)}, u32[]{:S(2)}) copy-start(f32[2048,128]{1,0:T(8,128)} %copy.27) | copy-start | bytes 3145732
  59.4 11.2 %collective-permute-start.1 = (bf16[16,32,128]{2,1,0:T(8,128)(2,1)S(1)}, bf16[16,32,128]{2,1,0:T(8,128)(2,1)S(1)}, u32[]{:S(2)}, u32[]{:S(2)}) collective-permute-start(bf16[16,32,128]{2,1,0:T(8,128)(2,1)S(1)} %fusion.25), channel_id=1, source_target_pairs={{0,2},{1,3},{2,0},{3,1},{4,6},{5,7},{6,4},{7,5},{8,10},{9,11},{10,... | collective-permute-start | bytes 393224 | tf_op jit(solution)/shard_map/ppermute | solution.py:138
  72.5 1.2 copy-start.6
  74.0 19.7 %collective-permute-start.3 = (bf16[512,512]{1,0:T(8,128)(2,1)}, bf16[512,512]{1,0:T(8,128)(2,1)}, u32[]{:S(2)}, u32[]{:S(2)}) collective-permute-start(bf16[512,512]{1,0:T(8,128)(2,1)} %get-tuple-element.19), channel_id=1, source_target_pairs={{0,15},{1,0},{2,1},{3,2},{4,3},{5,4},{6,5},{7,6},{8,7},{9,8},{10,9... | collective-permute-start | bytes 1572872 | tf_op jit(solution)/shard_map/ppermute | solution.py:194
  81.4 18.1 %collective-permute-start.2 = (bf16[512,512]{1,0:T(8,128)(2,1)}, bf16[512,512]{1,0:T(8,128)(2,1)}, u32[]{:S(2)}, u32[]{:S(2)}) collective-permute-start(bf16[512,512]{1,0:T(8,128)(2,1)} %get-tuple-element.20), channel_id=1, source_target_pairs={{0,1},{1,2},{2,3},{3,4},{4,5},{5,6},{6,7},{7,8},{8,9},{9,10},{10,1... | collective-permute-start | bytes 1572872 | tf_op jit(solution)/shard_map/ppermute | solution.py:193
  84.5 20.5 %collective-permute-start.5 = (bf16[512,512]{1,0:T(8,128)(2,1)}, bf16[512,512]{1,0:T(8,128)(2,1)}, u32[]{:S(2)}, u32[]{:S(2)}) collective-permute-start(bf16[512,512]{1,0:T(8,128)(2,1)} %get-tuple-element.20), channel_id=1, source_target_pairs={{0,15},{1,0},{2,1},{3,2},{4,3},{5,4},{6,5},{7,6},{8,7},{9,8},{10,9... | collective-permute-start | bytes 1572872 | tf_op jit(solution)/shard_map/ppermute | solution.py:198
  89.6 21.2 %collective-permute-start.4 = (bf16[512,512]{1,0:T(8,128)(2,1)}, bf16[512,512]{1,0:T(8,128)(2,1)}, u32[]{:S(2)}, u32[]{:S(2)}) collective-permute-start(bf16[512,512]{1,0:T(8,128)(2,1)} %get-tuple-element.19), channel_id=1, source_target_pairs={{0,1},{1,2},{2,3},{3,4},{4,5},{5,6},{6,7},{7,8},{8,9},{9,10},{10,1... | collective-permute-start | bytes 1572872 | tf_op jit(solution)/shard_map/ppermute | solution.py:197
  91.5 19.2 %copy-start.7 = (bf16[256,1024]{0,1:T(8,128)(2,1)S(1)}, bf16[256,1024]{0,1:T(8,128)(2,1)}, u32[]{:S(2)}) copy-start(bf16[256,1024]{0,1:T(8,128)(2,1)} %get-tuple-element.25) | copy-start | bytes 1572868
  93.7 22.5 %collective-permute-start.7 = (bf16[512,512]{1,0:T(8,128)(2,1)}, bf16[512,512]{1,0:T(8,128)(2,1)S(1)}, u32[]{:S(2)}, u32[]{:S(2)}) collective-permute-start(bf16[512,512]{1,0:T(8,128)(2,1)} %collective-permute-done.3), channel_id=1, source_target_pairs={{0,15},{1,0},{2,1},{3,2},{4,3},{5,4},{6,5},{7,6},{8,7},{9,8},{10,9... | collective-permute-start | bytes 1572872 | tf_op jit(solution)/shard_map/ppermute | solution.py:200
  99.5 22.4 %collective-permute-start.6 = (bf16[512,512]{1,0:T(8,128)(2,1)}, bf16[512,512]{1,0:T(8,128)(2,1)S(1)}, u32[]{:S(2)}, u32[]{:S(2)}) collective-permute-start(bf16[512,512]{1,0:T(8,128)(2,1)} %collective-permute-done.2), channel_id=1, source_target_pairs={{0,1},{1,2},{2,3},{3,4},{4,5},{5,6},{6,7},{7,8},{8,9},{9,10},{10,1... | collective-permute-start | bytes 1572872 | tf_op jit(solution)/shard_map/ppermute | solution.py:199
  101.4 10.7 %copy-start.8 = (f32[512,256]{1,0:T(8,128)S(1)}, f32[512,256]{1,0:T(8,128)}, u32[]{:S(2)}) copy-start(f32[512,256]{1,0:T(8,128)} %convolution_add_fusion.2) | copy-start | bytes 1572868
  112.1 9.8 %copy-start.9 = (bf16[1,512,256]{2,1,0:T(8,128)(2,1)S(1)}, bf16[1,512,256]{2,1,0:T(8,128)(2,1)}, u32[]{:S(2)}) copy-start(bf16[1,512,256]{2,1,0:T(8,128)(2,1)} %param.9) | copy-start | bytes 786436
  116.5 44.6 %copy-start.2 = (s32[128,8]{0,1:T(8,128)S(1)}, s32[128,8]{0,1:T(8,128)}, u32[]{:S(2)}) copy-start(s32[128,8]{0,1:T(8,128)} %param.7) | copy-start | bytes 12292
  116.5 44.6 %copy-start.4 = (f32[128,8]{0,1:T(8,128)S(1)}, f32[128,8]{0,1:T(8,128)}, u32[]{:S(2)}) copy-start(f32[128,8]{0,1:T(8,128)} %param.8) | copy-start | bytes 12292

commit v2 on v0

--- a/solution.py
+++ b/solution.py
@@ -176,38 +176,39 @@
     ).reshape(rows_total, padded)
     received, shared_part = lax.optimization_barrier((received, shared_part))
 
-    half = 4 * LANES
-    lower, upper = received[:, :half], received[:, half:class_width]
+    half = rows_total // 2
+    lower, upper = received[:half, :class_width], received[half:, :class_width]
     right = [(z, (z + 1) % local_count) for z in range(local_count)]
     left = [(z, (z - 1) % local_count) for z in range(local_count)]
     by_class = down_weight.reshape(quarter_width, -1, CLASSES, slice_width)
     by_class = by_class.transpose(2, 0, 1, 3).reshape(CLASSES, quarter_width, class_width)
 
-    def partial(rows, shift, part):
+    def partial(rows, shift):
         own_class = (lax.axis_index("local") + shift) % CLASSES
         weight = lax.dynamic_index_in_dim(by_class, own_class, 0, keepdims=False)
-        weight = weight[:, half:] if part else weight[:, :half]
         return lax.dot_general(rows, weight, (((1,), (1,)), ((), ())), preferred_element_type=jnp.float32)
 
     lower_left = lax.ppermute(lower, "local", right)
     upper_right = lax.ppermute(upper, "local", left)
-    hidden_grad = partial(lower, 0, 0) + partial(upper, 0, 1)
-    lower, upper, hidden_grad = lax.optimization_barrier((lower, upper, hidden_grad))
+    lower_grad, upper_grad = partial(lower, 0), partial(upper, 0)
+    lower, upper, lower_grad, upper_grad = lax.optimization_barrier((lower, upper, lower_grad, upper_grad))
     upper_left = lax.ppermute(upper, "local", right)
     lower_right = lax.ppermute(lower, "local", left)
     lower_far = lax.ppermute(lower_left, "local", right)
     upper_far = lax.ppermute(upper_right, "local", left)
-    hidden_grad = hidden_grad + partial(lower_left, CLASSES - 1, 0)
-    hidden_grad = hidden_grad + partial(upper_right, 1, 1)
-    hidden_grad = hidden_grad + partial(upper_left, CLASSES - 1, 1)
-    hidden_grad = hidden_grad + partial(lower_right, 1, 0)
-    hidden_grad = hidden_grad + partial(lower_far, 2, 0)
-    hidden_grad = hidden_grad + partial(upper_far, 2, 1)
+    lower_grad = lower_grad + partial(lower_left, CLASSES - 1) + partial(lower_right, 1)
+    upper_grad = upper_grad + partial(upper_right, 1) + partial(upper_left, CLASSES - 1)
+    lower_grad = lower_grad + partial(lower_far, 2)
+    upper_grad = upper_grad + partial(upper_far, 2)
     gate_column = lax.dynamic_slice_in_dim(received, class_width + own_expert, 1, 1).astype(jnp.float32)
-    expert_grad = (
-        (gate_column * hidden_grad).astype(jnp.bfloat16).reshape(1, rows_total, quarter_width)
-    )
-    slot_dots = jnp.sum(hidden_grad * saved_hidden[0].astype(jnp.float32), axis=1)
+    saved = saved_hidden[0].astype(jnp.float32)
+    experts, dots = [], []
+    for start, hidden_grad in ((0, lower_grad), (half, upper_grad)):
+        span = slice(start, start + half)
+        experts.append((gate_column[span] * hidden_grad).astype(jnp.bfloat16))
+        dots.append(jnp.sum(hidden_grad * saved[span], axis=1))
+    expert_grad = jnp.concatenate(experts, axis=0).reshape(1, rows_total, quarter_width)
+    slot_dots = jnp.concatenate(dots, axis=0)
 
     returned = lax.all_to_all(
         slot_dots.reshape(node_count, 1, capacity), "node", split_axis=0, concat_axis=0, tiled=True

time: 166 us -> 163 us (0.982)
  blocking collectives: 68.4 us -> 45.4 us
  waiting for transfers between devices: 28.2 us -> 38.7 us
  starting transfers between devices: 42.5 us -> 48.5 us
  local copies, waits for them, and re-layouts: 15.6 us -> 9.7 us
  other arithmetic: 0.3 us -> 4.73 us
  matrix products: 6.44 us -> 9.95 us
    all_to_all x1 -> x0, blocking collectives: 23 us -> none  [body(): lax.all_to_all(spread, 'local', split_axis=0, concat_axis=0, tiled=True)]
    all_to_all x0 -> x1, waiting for transfers between devices: none -> 14.8 us  [body(): lax.all_to_all(spread, 'local', split_axis=0, concat_axis=0, tiled=True)]
    ppermute x1, waiting for transfers between devices: 14.3 us -> 1.9 us  [body(): lower_far = lax.ppermute(lower_left, 'local', right)]
    all_to_all x0 -> x1, starting transfers between devices: none -> 6.75 us  [body(): lax.all_to_all(spread, 'local', split_axis=0, concat_axis=0, tiled=True)]
    ppermute x1, waiting for transfers between devices: 0.19 us -> 5.49 us  [body(): upper_far = lax.ppermute(upper_right, 'local', left)]
    ppermute x1, waiting for transfers between devices: 4.73 us -> 0.01 us  [body(): lower_left = lax.ppermute(lower, 'local', right)]
    ppermute x2, waiting for transfers between devices: 4.25 us -> 7.9 us  [swap_halves(): swapped = lax.ppermute(given, 'local', [(z, z ^ bit) for z in range(count)])]
    dot_general x8, matrix products: 6.1 us -> 9.63 us  [partial(): lax.dot_general(rows, weight, (((1,), (1,)), ((), ())), preferred_element...]
  transfers between devices with their start and end apart: 9 -> 10, of which waited for: 7 -> 8; matrix products, arithmetic and copies ran while one was open for 11% -> 10% of each run, Pallas kernels for 0% -> 0%
where the time goes in v2:
time: 163 us; the launch traced here: 162 us
  starting transfers between devices  48.5 us (30%)
  blocking collectives  45.4 us (28%)
  waiting for transfers between devices  38.7 us (24%)
  matrix products  9.95 us (6%)
  local copies, waits for them, and re-layouts  9.7 us (6%)
  other arithmetic  4.73 us (3%)
  Pallas kernels  3.82 us (2%)
    all_gather x1, blocking collectives, body(): lax.all_gather(grad_out.T, 'local', axis=0, tiled=True, axis_index_groups...  30.8 us
    all_to_all x1, waiting for transfers between devices, body(): lax.all_to_all(spread, 'local', split_axis=0, concat_axis=0, tiled=True)  14.8 us
    all_to_all x1, blocking collectives, body(): lax.all_to_all(slot_dots.reshape(node_count, 1, capacity), 'node', split_...  14.6 us
    all_to_all x1, starting transfers between devices, body(): lax.all_to_all(payload.reshape(node_count, capacity, padded), 'node', spl...  10.8 us
    dot_general x8, matrix products, partial(): lax.dot_general(rows, weight, (((1,), (1,)), ((), ())), preferred_element...  9.63 us
    ppermute x2, starting transfers between devices, swap_halves(): swapped = lax.ppermute(given, 'local', [(z, z ^ bit) for z in range(count)])  8.05 us
    ppermute x2, waiting for transfers between devices, swap_halves(): swapped = lax.ppermute(given, 'local', [(z, z ^ bit) for z in range(count)])  7.9 us
    all_to_all x1, starting transfers between devices, body(): lax.all_to_all(spread, 'local', split_axis=0, concat_axis=0, tiled=True)  6.75 us
  transfers between devices with their start and end apart: 10, of which 8 were waited for; matrix products, arithmetic and copies ran while one was open for 10% of the time, Pallas kernels for 0%

profile of v2, /device:TPU:2, one launch (start us, length us, event | category | flops | bytes accessed | tf_op | source)
XLA Modules:
  0.0 161.9 jit_solution(16495832439126912454)
XLA Ops:
  0.7 30.8 %all_gather.3.refs_0_ = bf16[896,128]{1,0:T(8,128)(2,1)S(1)} all-gather(bf16[224,128]{1,0:T(8,128)(2,1)} %bitcast.91), channel_id=1, replica_groups={{0,4,8,12},{1,5,9,13},{2,6,10,14},{3,7,11,15},{16,20,24,28},{17,21,25,2..., dimensions={0}, use_global_device_ids=true | all-gather | bytes 286720 | tf_op jit(solution)/shard_map/all_gather | solution.py:159
  32.8 1.9 %shard_map.85 = (bf16[512,1024]{1,0:T(8,128)(2,1)}, bf16[512,128]{1,0:T(8,128)(2,1)S(1)}) custom-call(bf16[896,128]{1,0:T(8,128)(2,1)S(1)} %all_gather.3.refs_0_, s32[8,128]{1,0:T(8,128)S(1)} %bitcast.74, f32[8,128]{1,0:T(8,128)S(1)} %bitcast.76), custom_call_target="tpu_custom_call" | custom-call | tf_op jit(solution)/shard_map/pallas_call | solution.py:160
  34.7 10.8 %all-to-all-start = ((bf16[64,8,1024]{2,1,0:T(8,128)(2,1)}), bf16[64,8,1024]{2,1,0:T(8,128)(2,1)}, u32[]{:S(2)}, u32[]{:S(2)}) async-start(bf16[64,8,1024]{2,1,0:T(8,128)(2,1)} %bitcast.3), calls=%async_computation | async-start | bytes 2097152 | tf_op jit(solution)/shard_map/all_to_all | solution.py:174
  46.3 3.1 %collective-permute-start = (bf16[16,64,128]{2,1,0:T(8,128)(2,1)S(1)}, bf16[16,64,128]{2,1,0:T(8,128)(2,1)S(1)}, u32[]{:S(2)}, u32[]{:S(2)}) collective-permute-start(bf16[16,64,128]{2,1,0:T(8,128)(2,1)S(1)} %fusion.22), channel_id=1, source_target_pairs={{0,1},{1,0},{2,3},{3,2},{4,5},{5,4},{6,7},{7,6},{8,9},{9,8},{10,11... | collective-permute-start | bytes 786440 | tf_op jit(solution)/shard_map/ppermute | solution.py:138
  49.5 7.1 %collective-permute-done = bf16[16,64,128]{2,1,0:T(8,128)(2,1)S(1)} collective-permute-done((bf16[16,64,128]{2,1,0:T(8,128)(2,1)S(1)}, bf16[16,64,128]{2,1,0:T(8,128)(2,1)S(1)}, u32[]{:S(2)}, u32[]{:S(2)}) %collective-permute-start) | collective-permute-done | bytes 262176 | tf_op jit(solution)/shard_map/ppermute | solution.py:138
  56.7 4.9 %collective-permute-start.1 = (bf16[16,32,128]{2,1,0:T(8,128)(2,1)S(1)}, bf16[16,32,128]{2,1,0:T(8,128)(2,1)}, u32[]{:S(2)}, u32[]{:S(2)}) collective-permute-start(bf16[16,32,128]{2,1,0:T(8,128)(2,1)S(1)} %fusion.28), channel_id=1, source_target_pairs={{0,2},{1,3},{2,0},{3,1},{4,6},{5,7},{6,4},{7,5},{8,10},{9,11},{10,... | collective-permute-start | bytes 393224 | tf_op jit(solution)/shard_map/ppermute | solution.py:138
  61.6 3.8 %copy.31 = bf16[256,3584]{0,1:T(8,128)(2,1)} copy(bf16[256,3584]{1,0:T(8,128)(2,1)} %param.10) | data formatting | bytes 3670016 | tf_op args[4]
  68.8 3.8 %all-to-all-done = bf16[64,8,1024]{2,1,0:T(8,128)(2,1)} async-done(((bf16[64,8,1024]{2,1,0:T(8,128)(2,1)}), bf16[64,8,1024]{2,1,0:T(8,128)(2,1)}, u32[]{:S(2)}, u32[]{:S(2)}) %all-to-all-start) | async-done | bytes 1048608 | tf_op jit(solution)/shard_map/all_to_all | solution.py:174
  72.6 2.0 %fusion.10 = f32[256,256]{1,0:T(8,128)} fusion(bf16[4,256,896]{1,2,0:T(8,128)(2,1)S(1)} %bitcast.78, s32[]{:T(128)S(6)} %select_n.87, bf16[512,1024]{1,0:T(8,128)(2,1)} %bitcast.4), kind=kOutput, calls=%fused_computation.17 | convolution fusion | flops 117440512 | bytes 1179652 | tf_op jit(solution)/shard_map/dot_general | solution.py:189
  74.6 2.0 %fusion.12 = f32[256,256]{1,0:T(8,128)} fusion(bf16[4,256,896]{1,2,0:T(8,128)(2,1)S(1)} %bitcast.79, s32[]{:T(128)S(6)} %select_n.87, bf16[512,1024]{1,0:T(8,128)(2,1)} %bitcast.4), kind=kOutput, calls=%fused_computation.19 | convolution fusion | flops 117440512 | bytes 1179652 | tf_op jit(solution)/shard_map/dot_general | solution.py:189
  76.7 2.2 %fusion.39 = (bf16[256,896]{1,0:T(8,128)(2,1)}, bf16[256,896]{1,0:T(8,128)(2,1)}) fusion(bf16[512,1024]{1,0:T(8,128)(2,1)} %bitcast.4), kind=kLoop, calls=%fused_computation.57 | loop fusion | bytes 1835008 | tf_op jit(solution)/shard_map/slice | solution.py:180
  78.8 3.1 %collective-permute-start.2 = (bf16[256,896]{1,0:T(8,128)(2,1)}, bf16[256,896]{1,0:T(8,128)(2,1)}, u32[]{:S(2)}, u32[]{:S(2)}) collective-permute-start(bf16[256,896]{1,0:T(8,128)(2,1)} %get-tuple-element.20), channel_id=1, source_target_pairs={{0,1},{1,2},{2,3},{3,4},{4,5},{5,6},{6,7},{7,8},{8,9},{9,10},{10,1... | collective-permute-start | bytes 1376264 | tf_op jit(solution)/shard_map/ppermute | solution.py:191
  81.9 6.2 %collective-permute-start.5 = (bf16[256,896]{1,0:T(8,128)(2,1)}, bf16[256,896]{1,0:T(8,128)(2,1)}, u32[]{:S(2)}, u32[]{:S(2)}) collective-permute-start(bf16[256,896]{1,0:T(8,128)(2,1)} %get-tuple-element.22), channel_id=1, source_target_pairs={{0,15},{1,0},{2,1},{3,2},{4,3},{5,4},{6,5},{7,6},{8,7},{9,8},{10,9... | collective-permute-start | bytes 1376264 | tf_op jit(solution)/shard_map/ppermute | solution.py:192
  88.2 3.9 %collective-permute-start.3 = (bf16[256,896]{1,0:T(8,128)(2,1)}, bf16[256,896]{1,0:T(8,128)(2,1)}, u32[]{:S(2)}, u32[]{:S(2)}) collective-permute-start(bf16[256,896]{1,0:T(8,128)(2,1)} %get-tuple-element.20), channel_id=1, source_target_pairs={{0,15},{1,0},{2,1},{3,2},{4,3},{5,4},{6,5},{7,6},{8,7},{9,8},{10,9... | collective-permute-start | bytes 1376264 | tf_op jit(solution)/shard_map/ppermute | solution.py:196
  93.2 2.1 %collective-permute-start.6 = (bf16[256,896]{1,0:T(8,128)(2,1)}, bf16[256,896]{1,0:T(8,128)(2,1)S(1)}, u32[]{:S(2)}, u32[]{:S(2)}) collective-permute-start(bf16[256,896]{1,0:T(8,128)(2,1)} %get-tuple-element.22), channel_id=1, source_target_pairs={{0,1},{1,2},{2,3},{3,4},{4,5},{5,6},{6,7},{7,8},{8,9},{9,10},{10,1... | collective-permute-start | bytes 1376264 | tf_op jit(solution)/shard_map/ppermute | solution.py:195
  96.4 2.6 %collective-permute-done.5 = bf16[256,896]{1,0:T(8,128)(2,1)} collective-permute-done((bf16[256,896]{1,0:T(8,128)(2,1)}, bf16[256,896]{1,0:T(8,128)(2,1)}, u32[]{:S(2)}, u32[]{:S(2)}) %collective-permute-start.5) | collective-permute-done | bytes 458784 | tf_op jit(solution)/shard_map/ppermute | solution.py:192
  99.0 5.6 %collective-permute-start.7 = (bf16[256,896]{1,0:T(8,128)(2,1)}, bf16[256,896]{1,0:T(8,128)(2,1)S(1)}, u32[]{:S(2)}, u32[]{:S(2)}) collective-permute-start(bf16[256,896]{1,0:T(8,128)(2,1)} %collective-permute-done.5), channel_id=1, source_target_pairs={{0,15},{1,0},{2,1},{3,2},{4,3},{5,4},{6,5},{7,6},{8,7},{9,8},{10,9... | collective-permute-start | bytes 1376264 | tf_op jit(solution)/shard_map/ppermute | solution.py:198
  104.6 1.9 %collective-permute-start.4 = (bf16[256,896]{1,0:T(8,128)(2,1)}, bf16[256,896]{1,0:T(8,128)(2,1)S(1)}, u32[]{:S(2)}, u32[]{:S(2)}) collective-permute-start(bf16[256,896]{1,0:T(8,128)(2,1)} %collective-permute-done.2), channel_id=1, source_target_pairs={{0,1},{1,2},{2,3},{3,4},{4,5},{5,6},{6,7},{7,8},{8,9},{9,10},{10,1... | collective-permute-start | bytes 1376264 | tf_op jit(solution)/shard_map/ppermute | solution.py:197
  106.6 2.3 %collective-permute-done.3 = bf16[256,896]{1,0:T(8,128)(2,1)} collective-permute-done((bf16[256,896]{1,0:T(8,128)(2,1)}, bf16[256,896]{1,0:T(8,128)(2,1)}, u32[]{:S(2)}, u32[]{:S(2)}) %collective-permute-start.3) | collective-permute-done | bytes 458784 | tf_op jit(solution)/shard_map/ppermute | solution.py:196
  113.2 5.5 %collective-permute-done.7 = bf16[256,896]{1,0:T(8,128)(2,1)S(1)} collective-permute-done((bf16[256,896]{1,0:T(8,128)(2,1)}, bf16[256,896]{1,0:T(8,128)(2,1)S(1)}, u32[]{:S(2)}, u32[]{:S(2)}) %collective-permute-start.7) | collective-permute-done | bytes 458784 | tf_op jit(solution)/shard_map/ppermute | solution.py:198
  119.0 1.9 %collective-permute-done.4 = bf16[256,896]{1,0:T(8,128)(2,1)S(1)} collective-permute-done((bf16[256,896]{1,0:T(8,128)(2,1)}, bf16[256,896]{1,0:T(8,128)(2,1)S(1)}, u32[]{:S(2)}, u32[]{:S(2)}) %collective-permute-start.4) | collective-permute-done | bytes 458784 | tf_op jit(solution)/shard_map/ppermute | solution.py:197
  122.2 14.6 %all_to_all.15.refs_0_ = f32[64,1,8]{2,1,0:T(1,128)S(1)} all-to-all(f32[64,1,8]{2,1,0:T(1,128)S(1)} %pad_maximum_fusion), channel_id=1, replica_groups=mesh['node'=64,'local'=16] {'node'}, dimensions={0} | all-to-all | bytes 4096 | tf_op jit(solution)/shard_map/all_to_all | solution.py:213
  137.7 6.7 %all-to-all-start.2 = ((bf16[16,48,128]{2,1,0:T(8,128)(2,1)}), bf16[16,48,128]{2,1,0:T(8,128)(2,1)S(1)}, u32[]{:S(2)}, u32[]{:S(2)}) async-start(bf16[16,48,128]{2,1,0:T(8,128)(2,1)} %shard_map.86), calls=%async_computation.2 | async-start | bytes 393216 | tf_op jit(solution)/shard_map/all_to_all | solution.py:225
  146.1 14.8 %all-to-all-done.2.refs_0_ = bf16[16,48,128]{2,1,0:T(8,128)(2,1)S(1)} async-done(((bf16[16,48,128]{2,1,0:T(8,128)(2,1)}), bf16[16,48,128]{2,1,0:T(8,128)(2,1)S(1)}, u32[]{:S(2)}, u32[]{:S(2)}) %all-to-all-start.2) | async-done | bytes 196640 | tf_op jit(solution)/shard_map/all_to_all | solution.py:225
  (41 shorter events, 17.2 us)
Async XLA Ops:
  0.6 45.0 %copy-start = (bf16[2048,224]{0,1:T(8,128)(2,1)S(1)}, bf16[2048,224]{0,1:T(8,128)(2,1)}, u32[]{:S(2)}) copy-start(bf16[2048,224]{0,1:T(8,128)(2,1)} %param.11) | copy-start | bytes 2752516
  0.6 45.0 %copy-start.7 = (bf16[128,224]{0,1:T(8,128)(2,1)S(1)}, bf16[128,224]{0,1:T(8,128)(2,1)}, u32[]{:S(2)}) copy-start(bf16[128,224]{0,1:T(8,128)(2,1)} %param.6) | copy-start | bytes 172036
  31.5 0.7 copy-start.1
  32.2 0.7 copy-start.3
  34.7 37.9 %all-to-all-start = ((bf16[64,8,1024]{2,1,0:T(8,128)(2,1)}), bf16[64,8,1024]{2,1,0:T(8,128)(2,1)}, u32[]{:S(2)}, u32[]{:S(2)}) async-start(bf16[64,8,1024]{2,1,0:T(8,128)(2,1)} %bitcast.3), calls=%async_computation | async-start | bytes 2097152 | tf_op jit(solution)/shard_map/all_to_all | solution.py:174
  46.3 10.3 %collective-permute-start = (bf16[16,64,128]{2,1,0:T(8,128)(2,1)S(1)}, bf16[16,64,128]{2,1,0:T(8,128)(2,1)S(1)}, u32[]{:S(2)}, u32[]{:S(2)}) collective-permute-start(bf16[16,64,128]{2,1,0:T(8,128)(2,1)S(1)} %fusion.22), channel_id=1, source_target_pairs={{0,1},{1,0},{2,3},{3,2},{4,5},{5,4},{6,7},{7,6},{8,9},{9,8},{10,11... | collective-permute-start | bytes 786440 | tf_op jit(solution)/shard_map/ppermute | solution.py:138
  56.7 11.2 %collective-permute-start.1 = (bf16[16,32,128]{2,1,0:T(8,128)(2,1)S(1)}, bf16[16,32,128]{2,1,0:T(8,128)(2,1)}, u32[]{:S(2)}, u32[]{:S(2)}) collective-permute-start(bf16[16,32,128]{2,1,0:T(8,128)(2,1)S(1)} %fusion.28), channel_id=1, source_target_pairs={{0,2},{1,3},{2,0},{3,1},{4,6},{5,7},{6,4},{7,5},{8,10},{9,11},{10,... | collective-permute-start | bytes 393224 | tf_op jit(solution)/shard_map/ppermute | solution.py:138
  78.8 25.8 %collective-permute-start.2 = (bf16[256,896]{1,0:T(8,128)(2,1)}, bf16[256,896]{1,0:T(8,128)(2,1)}, u32[]{:S(2)}, u32[]{:S(2)}) collective-permute-start(bf16[256,896]{1,0:T(8,128)(2,1)} %get-tuple-element.20), channel_id=1, source_target_pairs={{0,1},{1,2},{2,3},{3,4},{4,5},{5,6},{6,7},{7,8},{8,9},{9,10},{10,1... | collective-permute-start | bytes 1376264 | tf_op jit(solution)/shard_map/ppermute | solution.py:191
  81.9 17.1 %collective-permute-start.5 = (bf16[256,896]{1,0:T(8,128)(2,1)}, bf16[256,896]{1,0:T(8,128)(2,1)}, u32[]{:S(2)}, u32[]{:S(2)}) collective-permute-start(bf16[256,896]{1,0:T(8,128)(2,1)} %get-tuple-element.22), channel_id=1, source_target_pairs={{0,15},{1,0},{2,1},{3,2},{4,3},{5,4},{6,5},{7,6},{8,7},{9,8},{10,9... | collective-permute-start | bytes 1376264 | tf_op jit(solution)/shard_map/ppermute | solution.py:192
  88.2 20.7 %collective-permute-start.3 = (bf16[256,896]{1,0:T(8,128)(2,1)}, bf16[256,896]{1,0:T(8,128)(2,1)}, u32[]{:S(2)}, u32[]{:S(2)}) collective-permute-start(bf16[256,896]{1,0:T(8,128)(2,1)} %get-tuple-element.20), channel_id=1, source_target_pairs={{0,15},{1,0},{2,1},{3,2},{4,3},{5,4},{6,5},{7,6},{8,7},{9,8},{10,9... | collective-permute-start | bytes 1376264 | tf_op jit(solution)/shard_map/ppermute | solution.py:196
  93.2 17.0 %copy-start.6 = (f32[256,256]{1,0:T(8,128)S(1)}, f32[256,256]{1,0:T(8,128)}, u32[]{:S(2)}) copy-start(f32[256,256]{1,0:T(8,128)} %fusion.12) | copy-start | bytes 786436
  93.2 18.3 %collective-permute-start.6 = (bf16[256,896]{1,0:T(8,128)(2,1)}, bf16[256,896]{1,0:T(8,128)(2,1)S(1)}, u32[]{:S(2)}, u32[]{:S(2)}) collective-permute-start(bf16[256,896]{1,0:T(8,128)(2,1)} %get-tuple-element.22), channel_id=1, source_target_pairs={{0,1},{1,2},{2,3},{3,4},{4,5},{5,6},{6,7},{7,8},{8,9},{9,10},{10,1... | collective-permute-start | bytes 1376264 | tf_op jit(solution)/shard_map/ppermute | solution.py:195
  96.4 15.5 %copy-start.5 = (f32[256,256]{1,0:T(8,128)S(1)}, f32[256,256]{1,0:T(8,128)}, u32[]{:S(2)}) copy-start(f32[256,256]{1,0:T(8,128)} %fusion.10) | copy-start | bytes 786436
  99.0 19.7 %collective-permute-start.7 = (bf16[256,896]{1,0:T(8,128)(2,1)}, bf16[256,896]{1,0:T(8,128)(2,1)S(1)}, u32[]{:S(2)}, u32[]{:S(2)}) collective-permute-start(bf16[256,896]{1,0:T(8,128)(2,1)} %collective-permute-done.5), channel_id=1, source_target_pairs={{0,15},{1,0},{2,1},{3,2},{4,3},{5,4},{6,5},{7,6},{8,7},{9,8},{10,9... | collective-permute-start | bytes 1376264 | tf_op jit(solution)/shard_map/ppermute | solution.py:198
  104.6 16.3 %collective-permute-start.4 = (bf16[256,896]{1,0:T(8,128)(2,1)}, bf16[256,896]{1,0:T(8,128)(2,1)S(1)}, u32[]{:S(2)}, u32[]{:S(2)}) collective-permute-start(bf16[256,896]{1,0:T(8,128)(2,1)} %collective-permute-done.2), channel_id=1, source_target_pairs={{0,1},{1,2},{2,3},{3,4},{4,5},{5,6},{6,7},{7,8},{8,9},{9,10},{10,1... | collective-permute-start | bytes 1376264 | tf_op jit(solution)/shard_map/ppermute | solution.py:197
  119.0 41.9 %copy-start.2 = (s32[128,8]{0,1:T(8,128)S(1)}, s32[128,8]{0,1:T(8,128)}, u32[]{:S(2)}) copy-start(s32[128,8]{0,1:T(8,128)} %param.7) | copy-start | bytes 12292
  119.0 41.9 %copy-start.4 = (f32[128,8]{0,1:T(8,128)S(1)}, f32[128,8]{0,1:T(8,128)}, u32[]{:S(2)}) copy-start(f32[128,8]{0,1:T(8,128)} %param.8) | copy-start | bytes 12292
  137.7 23.2 %all-to-all-start.2 = ((bf16[16,48,128]{2,1,0:T(8,128)(2,1)}), bf16[16,48,128]{2,1,0:T(8,128)(2,1)S(1)}, u32[]{:S(2)}, u32[]{:S(2)}) async-start(bf16[16,48,128]{2,1,0:T(8,128)(2,1)} %shard_map.86), calls=%async_computation.2 | async-start | bytes 393216 | tf_op jit(solution)/shard_map/all_to_all | solution.py:225
